TPU v7x, 32 devices: a whole 2x2x4 slice. The times are simulated.
32 devices in a mesh: dp: 8 (over y, x, core), fsdp: 4 (over z).
Axes of the slice: x: 2, y: 2, z: 4, core: 2. Of those that a mesh axis runs over, the one named last changes fastest.
Arguments:
- owner_ids: int32 [16384, 8], P(('dp', 'fsdp')), may hold values from 0 to 31, all different within a row; in each aligned block of 512 rows (0 to 511, 512 to 1023, ...) at most 256 rows name the same one
- row_ids: int32 [16384, 8], P(('dp', 'fsdp')), may hold values from 0 to 4095
- embed_table: bfloat16 [131072, 64], P(('dp', 'fsdp')), may hold values from -6 to 6
- expandone: bfloat16 [3072, 256], P(('dp', 'fsdp')), may hold values from -0.25 to 0.25
- expbiasone: bfloat16 [1536], P(('dp', 'fsdp')), may hold values from -4 to 4
- reduceone: bfloat16 [1536, 256], P(('dp', 'fsdp')), may hold values from -0.375 to 0.375
- redbiasone: bfloat16 [1536], P(('dp', 'fsdp')), may hold values from -6 to 6
- normgainone: bfloat16 [1536], P(('dp', 'fsdp')), may hold values from 0.25 to 1.75
- taskgateone: bfloat16 [1024, 4], P(('dp', 'fsdp')), may hold values from -0.4375 to 0.4375
- sharegateone: bfloat16 [512, 6], P(('dp', 'fsdp')), may hold values from -0.4375 to 0.4375
- expandtwo: bfloat16 [1536, 256], P(('dp', 'fsdp')), may hold values from -0.375 to 0.375
- expbiastwo: bfloat16 [1536], P(('dp', 'fsdp')), may hold values from -4 to 4
- reducetwo: bfloat16 [1536, 256], P(('dp', 'fsdp')), may hold values from -0.375 to 0.375
- redbiastwo: bfloat16 [1536], P(('dp', 'fsdp')), may hold values from -6 to 6
- normgaintwo: bfloat16 [1536], P(('dp', 'fsdp')), may hold values from 0.25 to 1.75
- taskgatetwo: bfloat16 [512, 4], P(('dp', 'fsdp')), may hold values from -1 to 1
- towerinner: bfloat16 [512, 128], P(('dp', 'fsdp')), may hold values from -0.375 to 0.375
- towerbias: bfloat16 [256], P(('dp', 'fsdp')), may hold values from -4 to 4
- towermiddle: bfloat16 [256, 64], P(('dp', 'fsdp')), may hold values from -0.5 to 0.5
- towertail: bfloat16 [256], P(('dp', 'fsdp')), may hold values from -4 to 4
- logit_cot: float32 [2, 16384], P(None, ('dp', 'fsdp')), may hold values from -6 to 6
Outputs:
- logits: float32 [2, 16384], P(None, ('dp', 'fsdp'))
- x_grad: float32 [16384, 512], P(('dp', 'fsdp'))
- embed_table_grad: float32 [131072, 64], P(('dp', 'fsdp'))
- expandone_grad: float32 [3072, 256], replicated
- expbiasone_grad: float32 [1536], replicated
- reduceone_grad: float32 [1536, 256], replicated
- redbiasone_grad: float32 [1536], replicated
- normgainone_grad: float32 [1536], replicated
- taskgateone_grad: float32 [1024, 4], replicated
- sharegateone_grad: float32 [512, 6], replicated
- expandtwo_grad: float32 [1536, 256], replicated
- expbiastwo_grad: float32 [1536], replicated
- reducetwo_grad: float32 [1536, 256], replicated
- redbiastwo_grad: float32 [1536], replicated
- normgaintwo_grad: float32 [1536], replicated
- taskgatetwo_grad: float32 [512, 4], replicated
- towerinner_grad: float32 [512, 128], replicated
- towerbias_grad: float32 [256], replicated
- towermiddle_grad: float32 [256, 64], replicated
- towertail_grad: float32 [256], replicated
Inputs may be any that keep to these rules, and one draw needn't show every extreme that they name: `owner_ids`: an event's 8 owners are different. Among the lookups of one device's events, no owner is named more than 256 times, a bound that some block reaches.
All inputs are finite; a program needn't handle non-finite values.
Results may differ from a plain program's by a relative error of at most 0.017.
Values may be sent and summed in bfloat16 or wider, within the bound.
No kernel may reach another device: no remote copies, remote signals or barrier semaphores. Data moves between devices by JAX's collectives and lax.ppermute only.
A program may use at most 128 MiB of HBM per device.

v0:
```python
import jax
import jax.numpy as jnp
from jax import lax
from jax.sharding import PartitionSpec as P

EPS = 1e-05


def silu_slope(values):
    sigmoid_v = jax.nn.sigmoid(values)
    return sigmoid_v * (1.0 + values * (1.0 - sigmoid_v))


def expert_forward(inputs, pattern, expand, expbias, shrink, shrinkbias, gain_w):
    hidden = shrink.shape[1]
    in_width = expand.shape[0] // 6
    expand_w = expand.reshape(3, 2, in_width, hidden)
    preact = jnp.einsum(
        pattern, inputs, expand_w, preferred_element_type=jnp.float32
    ) + expbias.astype(jnp.float32).reshape(3, 2, 1, hidden)
    active = jax.nn.silu(preact).astype(jnp.bfloat16)
    output = jnp.einsum(
        "gknh,gkho->gkno",
        active,
        shrink.reshape(3, 2, hidden, hidden),
        preferred_element_type=jnp.float32,
    ) + shrinkbias.astype(jnp.float32).reshape(3, 2, 1, hidden)
    centered = output - jnp.mean(output, axis=-1, keepdims=True)
    inverse = lax.rsqrt(jnp.mean(centered * centered, axis=-1, keepdims=True) + EPS)
    normed = centered * inverse
    result = normed * gain_w.astype(jnp.float32).reshape(3, 2, 1, hidden)
    return (result, (preact, active, normed, inverse))


def expert_backward(inputs, level_first, expand, shrink, gain_w, saved_parts, upstream):
    preact, active, normed, inverse = saved_parts
    hidden = shrink.shape[1]
    in_width = expand.shape[0] // 6
    scaled = upstream * gain_w.astype(jnp.float32).reshape(3, 2, 1, hidden)
    gain_grad = jnp.sum(upstream * normed, axis=2)
    out_grad = inverse * (
        scaled
        - jnp.mean(scaled, axis=-1, keepdims=True)
        - normed * jnp.mean(scaled * normed, axis=-1, keepdims=True)
    )
    out_low = out_grad.astype(jnp.bfloat16)
    shrinkbias_grad = jnp.sum(out_low.astype(jnp.float32), axis=2)
    shrink_grad = jnp.einsum("gknh,gkno->gkho", active, out_low, preferred_element_type=jnp.float32)
    act_grad = jnp.einsum(
        "gkno,gkho->gknh",
        out_low,
        shrink.reshape(3, 2, hidden, hidden),
        preferred_element_type=jnp.float32,
    )
    pre_low = (act_grad * silu_slope(preact)).astype(jnp.bfloat16)
    expbias_grad = jnp.sum(pre_low.astype(jnp.float32), axis=2)
    expand_w = expand.reshape(3, 2, in_width, hidden)
    if level_first:
        expand_grad = jnp.einsum(
            "nd,gknh->gkdh", inputs, pre_low, preferred_element_type=jnp.float32
        )
        input_grad = jnp.einsum(
            "gknh,gkdh->nd", pre_low, expand_w, preferred_element_type=jnp.float32
        )
    else:
        expand_grad = jnp.einsum(
            "gnd,gknh->gkdh", inputs, pre_low, preferred_element_type=jnp.float32
        )
        input_grad = jnp.einsum(
            "gknh,gkdh->gnd", pre_low, expand_w, preferred_element_type=jnp.float32
        )
    weight_grads = (
        expand_grad.reshape(6 * in_width, hidden),
        expbias_grad.reshape(-1),
        shrink_grad.reshape(6 * hidden, hidden),
        shrinkbias_grad.reshape(-1),
        gain_grad.reshape(-1),
    )
    return (weight_grads, input_grad)


def gate_forward(inputs, gate_w):
    scores = jnp.einsum("nd,dk->kn", inputs, gate_w, preferred_element_type=jnp.float32)
    return jax.nn.softmax(scores, axis=0)


def mix_forward(task_probs, pieces):
    return jnp.sum(task_probs[:, :, None] * pieces, axis=0)


def mix_backward(task_probs, pieces, upstream):
    piece_grad = task_probs[:, :, None] * upstream[None]
    prob_grad = jnp.sum(pieces * upstream[None], axis=-1)
    score_grad = task_probs * (prob_grad - jnp.sum(task_probs * prob_grad, axis=0, keepdims=True))
    return (piece_grad, score_grad.astype(jnp.bfloat16))


def on_device(
    owner_ids,
    row_ids,
    embed_table,
    expandone,
    expbiasone,
    reduceone,
    redbiasone,
    normgainone,
    taskgateone,
    sharegateone,
    expandtwo,
    expbiastwo,
    reducetwo,
    redbiastwo,
    normgaintwo,
    taskgatetwo,
    towerinner,
    towerbias,
    towermiddle,
    towertail,
    logit_cot,
):
    devices = lax.axis_size(("dp", "fsdp"))
    events, fields = owner_ids.shape
    emb_width = embed_table.shape[1]
    capacity = 2 * events * fields // devices
    owner_flat = owner_ids.reshape(-1)
    owner_hits = (owner_flat[:, None] == jnp.arange(devices, dtype=jnp.int32)[None, :]).astype(
        jnp.int32
    )
    slot_rank = jnp.sum((jnp.cumsum(owner_hits, axis=0) - 1) * owner_hits, axis=1)
    position = owner_flat * capacity + slot_rank
    request = (
        jnp.zeros((devices * capacity,), jnp.int32)
        .at[position]
        .set(row_ids.reshape(-1))
        .reshape(devices, capacity)
    )
    asked_rows = lax.all_to_all(request, ("dp", "fsdp"), split_axis=0, concat_axis=0, tiled=True)
    found_rows = jnp.take(embed_table, asked_rows.reshape(-1), axis=0).reshape(
        devices, capacity, emb_width
    )
    returned = lax.all_to_all(found_rows, ("dp", "fsdp"), split_axis=0, concat_axis=0, tiled=True)
    features = jnp.take(returned.reshape(-1, emb_width), position, axis=0).reshape(
        events, fields * emb_width
    )
    one_expand, one_inbias, one_shrink, one_outbias, one_gain, one_taskgate, one_sharegate = (
        lax.all_gather(expandone, ("dp", "fsdp"), axis=0, tiled=True),
        lax.all_gather(expbiasone, ("dp", "fsdp"), axis=0, tiled=True),
        lax.all_gather(reduceone, ("dp", "fsdp"), axis=0, tiled=True),
        lax.all_gather(redbiasone, ("dp", "fsdp"), axis=0, tiled=True),
        lax.all_gather(normgainone, ("dp", "fsdp"), axis=0, tiled=True),
        lax.all_gather(taskgateone, ("dp", "fsdp"), axis=0, tiled=True),
        lax.all_gather(sharegateone, ("dp", "fsdp"), axis=0, tiled=True),
    )
    (
        two_expand,
        two_inbias,
        two_shrink,
        two_outbias,
        two_gain,
        two_taskgate,
        inner_full,
        tbias_full,
        middle_full,
        tail_full,
    ) = (
        lax.all_gather(expandtwo, ("dp", "fsdp"), axis=0, tiled=True),
        lax.all_gather(expbiastwo, ("dp", "fsdp"), axis=0, tiled=True),
        lax.all_gather(reducetwo, ("dp", "fsdp"), axis=0, tiled=True),
        lax.all_gather(redbiastwo, ("dp", "fsdp"), axis=0, tiled=True),
        lax.all_gather(normgaintwo, ("dp", "fsdp"), axis=0, tiled=True),
        lax.all_gather(taskgatetwo, ("dp", "fsdp"), axis=0, tiled=True),
        lax.all_gather(towerinner, ("dp", "fsdp"), axis=0, tiled=True),
        lax.all_gather(towerbias, ("dp", "fsdp"), axis=0, tiled=True),
        lax.all_gather(towermiddle, ("dp", "fsdp"), axis=0, tiled=True),
        lax.all_gather(towertail, ("dp", "fsdp"), axis=0, tiled=True),
    )
    in_width = features.shape[1]
    hidden = one_shrink.shape[1]
    first_out, first_saved = expert_forward(
        features, "nd,gkdh->gknh", one_expand, one_inbias, one_shrink, one_outbias, one_gain
    )
    lower_gates = one_taskgate.reshape(2, in_width, 4)
    first_probs = [gate_forward(features, lower_gates[task_index]) for task_index in range(2)]
    shared_probs = gate_forward(features, one_sharegate)
    first_pieces = [
        jnp.concatenate([first_out[task_index], first_out[2]], axis=0) for task_index in range(2)
    ]
    first_flat = first_out.reshape(6, events, hidden)
    carried = jnp.stack(
        [
            mix_forward(first_probs[0], first_pieces[0]),
            mix_forward(first_probs[1], first_pieces[1]),
            mix_forward(shared_probs, first_flat),
        ]
    ).astype(jnp.bfloat16)
    second_out, second_saved = expert_forward(
        carried, "gnd,gkdh->gknh", two_expand, two_inbias, two_shrink, two_outbias, two_gain
    )
    upper_gates = two_taskgate.reshape(2, hidden, 4)
    second_probs = [
        gate_forward(carried[task_index], upper_gates[task_index]) for task_index in range(2)
    ]
    second_pieces = [
        jnp.concatenate([second_out[task_index], second_out[2]], axis=0) for task_index in range(2)
    ]
    tower_input = jnp.stack(
        [
            mix_forward(second_probs[task_index], second_pieces[task_index])
            for task_index in range(2)
        ]
    ).astype(jnp.bfloat16)
    inner_w = inner_full.reshape(2, hidden, -1)
    first_tower = jnp.einsum(
        "tnd,tdh->tnh", tower_input, inner_w, preferred_element_type=jnp.float32
    ) + tbias_full.astype(jnp.float32).reshape(2, 1, -1)
    tower_act = jax.nn.silu(first_tower).astype(jnp.bfloat16)
    middle_w = middle_full.reshape(2, inner_w.shape[2], -1)
    narrow = middle_w.shape[2]
    tail_parts = tail_full.astype(jnp.float32).reshape(2, 2, narrow)
    second_tower = (
        jnp.einsum("tnh,thk->tkn", tower_act, middle_w, preferred_element_type=jnp.float32)
        + tail_parts[:, 0, :, None]
    )
    tower_top = jax.nn.silu(second_tower)
    logits = jnp.sum(tower_top * tail_parts[:, 1, :, None], axis=1)
    top_grad = (
        logit_cot[:, None, :] * tail_parts[:, 1, :, None] * silu_slope(second_tower)
    ).astype(jnp.bfloat16)
    tail_grad = jnp.stack(
        [
            jnp.sum(top_grad.astype(jnp.float32), axis=2),
            jnp.sum(tower_top * logit_cot[:, None, :], axis=2),
        ],
        axis=1,
    ).reshape(-1)
    middle_grad = jnp.einsum(
        "tnh,tkn->thk", tower_act, top_grad, preferred_element_type=jnp.float32
    ).reshape(-1, narrow)
    tower_act_grad = jnp.einsum(
        "tkn,thk->tnh", top_grad, middle_w, preferred_element_type=jnp.float32
    )
    first_grad = (tower_act_grad * silu_slope(first_tower)).astype(jnp.bfloat16)
    tbias_grad = jnp.sum(first_grad.astype(jnp.float32), axis=1).reshape(-1)
    inner_grad = jnp.einsum(
        "tnd,tnh->tdh", tower_input, first_grad, preferred_element_type=jnp.float32
    ).reshape(-1, inner_w.shape[2])
    tower_in_grad = jnp.einsum(
        "tnh,tdh->tnd", first_grad, inner_w, preferred_element_type=jnp.float32
    )
    second_piece_grads = []
    two_gate_grads = []
    gate_side_grads = []
    for task_index in range(2):
        piece_grad, score_low = mix_backward(
            second_probs[task_index], second_pieces[task_index], tower_in_grad[task_index]
        )
        second_piece_grads.append(piece_grad)
        two_gate_grads.append(
            jnp.einsum(
                "nd,kn->dk", carried[task_index], score_low, preferred_element_type=jnp.float32
            )
        )
        gate_side_grads.append(
            jnp.einsum(
                "kn,dk->nd", score_low, upper_gates[task_index], preferred_element_type=jnp.float32
            )
        )
    second_upstream = jnp.stack(
        [
            second_piece_grads[0][:2],
            second_piece_grads[1][:2],
            second_piece_grads[0][2:] + second_piece_grads[1][2:],
        ]
    )
    second_grads, second_in_grad = expert_backward(
        carried, False, two_expand, two_shrink, two_gain, second_saved, second_upstream
    )
    carried_total = second_in_grad + jnp.stack(
        [gate_side_grads[0], gate_side_grads[1], jnp.zeros_like(gate_side_grads[0])]
    )
    up_expand, up_inbias, up_shrink, up_outbias, up_gain = second_grads
    up_taskgate = jnp.concatenate(two_gate_grads, axis=0)
    first_piece_grads = []
    one_gate_grads = []
    feature_grad = jnp.zeros((events, in_width), jnp.float32)
    for task_index in range(2):
        piece_grad, score_low = mix_backward(
            first_probs[task_index], first_pieces[task_index], carried_total[task_index]
        )
        first_piece_grads.append(piece_grad)
        one_gate_grads.append(
            jnp.einsum("nd,kn->dk", features, score_low, preferred_element_type=jnp.float32)
        )
        feature_grad = feature_grad + jnp.einsum(
            "kn,dk->nd", score_low, lower_gates[task_index], preferred_element_type=jnp.float32
        )
    shared_piece_grad, shared_low = mix_backward(shared_probs, first_flat, carried_total[2])
    low_sharegate = jnp.einsum(
        "nd,kn->dk", features, shared_low, preferred_element_type=jnp.float32
    )
    feature_grad = feature_grad + jnp.einsum(
        "kn,dk->nd", shared_low, one_sharegate, preferred_element_type=jnp.float32
    )
    first_upstream = shared_piece_grad.reshape(3, 2, events, hidden) + jnp.stack(
        [
            first_piece_grads[0][:2],
            first_piece_grads[1][:2],
            first_piece_grads[0][2:] + first_piece_grads[1][2:],
        ]
    )
    first_grads, expert_feature_grad = expert_backward(
        features, True, one_expand, one_shrink, one_gain, first_saved, first_upstream
    )
    x_grad = expert_feature_grad + feature_grad
    low_expand, low_inbias, low_shrink, low_outbias, low_gain = first_grads
    low_taskgate = jnp.concatenate(one_gate_grads, axis=0)
    outgoing = (
        jnp.zeros((devices * capacity, emb_width), jnp.float32)
        .at[position]
        .set(x_grad.reshape(-1, emb_width))
        .reshape(devices, capacity, emb_width)
    )
    incoming = lax.all_to_all(
        outgoing.astype(jnp.bfloat16), ("dp", "fsdp"), split_axis=0, concat_axis=0, tiled=True
    ).astype(outgoing.dtype)
    table_grad = (
        jnp.zeros((embed_table.shape[0], emb_width), jnp.float32)
        .at[asked_rows.reshape(-1)]
        .add(incoming.reshape(-1, emb_width))
    )
    all_part = (
        lax.psum_scatter(low_expand, ("dp", "fsdp"), scatter_dimension=0, tiled=True),
        lax.psum_scatter(low_inbias, ("dp", "fsdp"), scatter_dimension=0, tiled=True),
        lax.psum_scatter(low_shrink, ("dp", "fsdp"), scatter_dimension=0, tiled=True),
        lax.psum_scatter(low_outbias, ("dp", "fsdp"), scatter_dimension=0, tiled=True),
        lax.psum_scatter(low_gain, ("dp", "fsdp"), scatter_dimension=0, tiled=True),
        lax.psum_scatter(low_taskgate, ("dp", "fsdp"), scatter_dimension=0, tiled=True),
        lax.psum_scatter(low_sharegate, ("dp", "fsdp"), scatter_dimension=0, tiled=True),
        lax.psum_scatter(up_expand, ("dp", "fsdp"), scatter_dimension=0, tiled=True),
        lax.psum_scatter(up_inbias, ("dp", "fsdp"), scatter_dimension=0, tiled=True),
        lax.psum_scatter(up_shrink, ("dp", "fsdp"), scatter_dimension=0, tiled=True),
        lax.psum_scatter(up_outbias, ("dp", "fsdp"), scatter_dimension=0, tiled=True),
        lax.psum_scatter(up_gain, ("dp", "fsdp"), scatter_dimension=0, tiled=True),
        lax.psum_scatter(up_taskgate, ("dp", "fsdp"), scatter_dimension=0, tiled=True),
        lax.psum_scatter(inner_grad, ("dp", "fsdp"), scatter_dimension=0, tiled=True),
        lax.psum_scatter(tbias_grad, ("dp", "fsdp"), scatter_dimension=0, tiled=True),
        lax.psum_scatter(middle_grad, ("dp", "fsdp"), scatter_dimension=0, tiled=True),
        lax.psum_scatter(tail_grad, ("dp", "fsdp"), scatter_dimension=0, tiled=True),
    )
    (
        a_expand,
        a_inbias,
        a_shrink,
        a_outbias,
        a_gain,
        a_taskgate,
        a_sharegate,
        b_expand,
        b_inbias,
        b_shrink,
        b_outbias,
        b_gain,
        b_taskgate,
        b_inner,
        b_tbias,
        b_middle,
        b_tail,
    ) = all_part
    all_done = (
        lax.all_gather(a_expand.astype(jnp.bfloat16), ("dp", "fsdp"), axis=0, tiled=True).astype(
            a_expand.dtype
        ),
        lax.all_gather(a_inbias.astype(jnp.bfloat16), ("dp", "fsdp"), axis=0, tiled=True).astype(
            a_inbias.dtype
        ),
        lax.all_gather(a_shrink.astype(jnp.bfloat16), ("dp", "fsdp"), axis=0, tiled=True).astype(
            a_shrink.dtype
        ),
        lax.all_gather(a_outbias.astype(jnp.bfloat16), ("dp", "fsdp"), axis=0, tiled=True).astype(
            a_outbias.dtype
        ),
        lax.all_gather(a_gain.astype(jnp.bfloat16), ("dp", "fsdp"), axis=0, tiled=True).astype(
            a_gain.dtype
        ),
        lax.all_gather(a_taskgate.astype(jnp.bfloat16), ("dp", "fsdp"), axis=0, tiled=True).astype(
            a_taskgate.dtype
        ),
        lax.all_gather(a_sharegate.astype(jnp.bfloat16), ("dp", "fsdp"), axis=0, tiled=True).astype(
            a_sharegate.dtype
        ),
        lax.all_gather(b_expand.astype(jnp.bfloat16), ("dp", "fsdp"), axis=0, tiled=True).astype(
            b_expand.dtype
        ),
        lax.all_gather(b_inbias.astype(jnp.bfloat16), ("dp", "fsdp"), axis=0, tiled=True).astype(
            b_inbias.dtype
        ),
        lax.all_gather(b_shrink.astype(jnp.bfloat16), ("dp", "fsdp"), axis=0, tiled=True).astype(
            b_shrink.dtype
        ),
        lax.all_gather(b_outbias.astype(jnp.bfloat16), ("dp", "fsdp"), axis=0, tiled=True).astype(
            b_outbias.dtype
        ),
        lax.all_gather(b_gain.astype(jnp.bfloat16), ("dp", "fsdp"), axis=0, tiled=True).astype(
            b_gain.dtype
        ),
        lax.all_gather(b_taskgate.astype(jnp.bfloat16), ("dp", "fsdp"), axis=0, tiled=True).astype(
            b_taskgate.dtype
        ),
        lax.all_gather(b_inner.astype(jnp.bfloat16), ("dp", "fsdp"), axis=0, tiled=True).astype(
            b_inner.dtype
        ),
        lax.all_gather(b_tbias.astype(jnp.bfloat16), ("dp", "fsdp"), axis=0, tiled=True).astype(
            b_tbias.dtype
        ),
        lax.all_gather(b_middle.astype(jnp.bfloat16), ("dp", "fsdp"), axis=0, tiled=True).astype(
            b_middle.dtype
        ),
        lax.all_gather(b_tail.astype(jnp.bfloat16), ("dp", "fsdp"), axis=0, tiled=True).astype(
            b_tail.dtype
        ),
    )
    lower_done = all_done[:7]
    upper_done = all_done[7:]
    return (
        logits,
        x_grad,
        table_grad,
        lower_done[0],
        lower_done[1],
        lower_done[2],
        lower_done[3],
        lower_done[4],
        lower_done[5],
        lower_done[6],
        upper_done[0],
        upper_done[1],
        upper_done[2],
        upper_done[3],
        upper_done[4],
        upper_done[5],
        upper_done[6],
        upper_done[7],
        upper_done[8],
        upper_done[9],
    )


def solution(mesh):
    return jax.shard_map(
        on_device,
        mesh=mesh,
        in_specs=(
            P(("dp", "fsdp"), None),
            P(("dp", "fsdp"), None),
            P(("dp", "fsdp"), None),
            P(("dp", "fsdp"), None),
            P(("dp", "fsdp")),
            P(("dp", "fsdp"), None),
            P(("dp", "fsdp")),
            P(("dp", "fsdp")),
            P(("dp", "fsdp"), None),
            P(("dp", "fsdp"), None),
            P(("dp", "fsdp"), None),
            P(("dp", "fsdp")),
            P(("dp", "fsdp"), None),
            P(("dp", "fsdp")),
            P(("dp", "fsdp")),
            P(("dp", "fsdp"), None),
            P(("dp", "fsdp"), None),
            P(("dp", "fsdp")),
            P(("dp", "fsdp"), None),
            P(("dp", "fsdp")),
            P(None, ("dp", "fsdp")),
        ),
        out_specs=(
            P(None, ("dp", "fsdp")),
            P(("dp", "fsdp"), None),
            P(("dp", "fsdp"), None),
            P(),
            P(),
            P(),
            P(),
            P(),
            P(),
            P(),
            P(),
            P(),
            P(),
            P(),
            P(),
            P(),
            P(),
            P(),
            P(),
            P(),
        ),
        check_vma=False,
    )
```

profile of v0, /device:TPU:0, one launch (start us, length us, event | category | flops | bytes accessed | tf_op | source)
XLA Modules:
  0.0 1830.9 jit_solution(5839908885962677692)
XLA Ops:
  11.3 9.2 reduce-window.6
  22.1 16.1 scatter_custom_fusion
  38.2 7.3 all-to-all-start
  47.7 40.9 %all-reduce.27 = (bf16[1536]{0:T(1024)(128)(2,1)S(1)}, bf16[1536]{0:T(1024)(128)(2,1)S(1)}, bf16[1536]{0:T(1024)(128)(2,1)S(1)}, bf16[1536]{0:T(1024)(128)(2,1)S...) all-reduce(bf16[1536]{0:T(1024)(128)(2,1)S(1)} %dynamic-update-slic, ...), channel_id=1, replica_groups=mesh['dp'=8,'fsdp'=4] {'dp','fsdp'}, use_global_device_ids=true, to_apply=%add.5 | all-reduce | flops 9728 | bytes 38912
  91.2 66.1 %all-gather = bf16[32,32,4]{1,2,0:T(4,128)(2,1)S(1)} all-gather(bf16[1,32,4]{1,2,0:T(4,128)(2,1)S(1)} %bitcast.370), channel_id=1, replica_groups=mesh['dp'=8,'fsdp'=4] {'dp','fsdp'}, dimensions={0}, use_global_device_ids=true | all-gather | bytes 8448 | tf_op jit(solution)/shard_map/all_gather | solution.py:151
  157.6 63.5 %all-gather.1 = bf16[32,16,4]{1,2,0:T(4,128)(2,1)S(1)} all-gather(bf16[1,16,4]{1,2,0:T(4,128)(2,1)S(1)} %bitcast.371), channel_id=1, replica_groups=mesh['dp'=8,'fsdp'=4] {'dp','fsdp'}, dimensions={0}, use_global_device_ids=true | all-gather | bytes 4224 | tf_op jit(solution)/shard_map/all_gather | solution.py:171
  222.4 66.0 %all-gather.2 = bf16[32,16,6]{1,2,0:T(8,128)(2,1)S(1)} all-gather(bf16[1,16,6]{1,2,0:T(8,128)(2,1)S(1)} %bitcast.368), channel_id=1, replica_groups=mesh['dp'=8,'fsdp'=4] {'dp','fsdp'}, dimensions={0}, use_global_device_ids=true | all-gather | bytes 6336 | tf_op jit(solution)/shard_map/all_gather | solution.py:152
  288.6 68.5 %all_gather.117 = bf16[256,64]{1,0:T(8,128)(2,1)} all-gather(bf16[8,64]{1,0:T(8,128)(2,1)S(1)} %copy-done.108), channel_id=1, replica_groups=mesh['dp'=8,'fsdp'=4] {'dp','fsdp'}, dimensions={0}, use_global_device_ids=true | all-gather | bytes 33792 | tf_op jit(solution)/shard_map/all_gather | solution.py:174
  358.4 65.5 %all_gather.115 = bf16[512,128]{1,0:T(8,128)(2,1)S(1)} all-gather(bf16[16,128]{1,0:T(8,128)(2,1)S(1)} %copy-done.106), channel_id=1, replica_groups=mesh['dp'=8,'fsdp'=4] {'dp','fsdp'}, dimensions={0}, use_global_device_ids=true | all-gather | bytes 135168 | tf_op jit(solution)/shard_map/all_gather | solution.py:172
  424.0 24.0 %gather_fusion = bf16[8192,64]{1,0:T(8,128)(2,1)S(1)} fusion(bf16[4096,64]{1,0:T(8,128)(2,1)S(1)} %copy.209, s32[8192]{0:T(1024)S(1)} %broadcast_clamp_fusion), kind=kCustom, calls=%fused_computation | custom fusion | bytes 2129920 | tf_op jit(solution)/shard_map/jit(_take)/gather | solution.py:138
  450.0 2.6 all-to-all-start.1
  453.9 94.8 %all_gather.105 = bf16[1536,256]{1,0:T(8,128)(2,1)} all-gather(bf16[48,256]{1,0:T(8,128)(2,1)S(1)} %copy-done.93), channel_id=1, replica_groups=mesh['dp'=8,'fsdp'=4] {'dp','fsdp'}, dimensions={0}, use_global_device_ids=true | all-gather | bytes 811008 | tf_op jit(solution)/shard_map/all_gather | solution.py:148
  548.7 75.8 %all_gather.110 = bf16[1536,256]{1,0:T(8,128)(2,1)} all-gather(bf16[48,256]{1,0:T(8,128)(2,1)S(1)} %copy-done.94), channel_id=1, replica_groups=mesh['dp'=8,'fsdp'=4] {'dp','fsdp'}, dimensions={0}, use_global_device_ids=true | all-gather | bytes 811008 | tf_op jit(solution)/shard_map/all_gather | solution.py:166
  624.4 76.8 %all_gather.112 = bf16[1536,256]{1,0:T(8,128)(2,1)} all-gather(bf16[48,256]{1,0:T(8,128)(2,1)S(1)} %copy-done.95), channel_id=1, replica_groups=mesh['dp'=8,'fsdp'=4] {'dp','fsdp'}, dimensions={0}, use_global_device_ids=true | all-gather | bytes 811008 | tf_op jit(solution)/shard_map/all_gather | solution.py:168
  702.3 12.1 gather_fusion.1
  718.2 4.5 fusion.11
  724.1 3.2 multiply_reduce_fusion.6
  739.5 4.0 fusion.3
  762.5 2.9 multiply_reduce_fusion.13
  770.4 2.5 convert_reduce_fusion
  783.7 2.9 multiply_reduce_fusion.10
  788.6 3.0 multiply_reduce_fusion.1
  791.7 2.6 convert_reduce_fusion.2
  796.1 2.7 convolution_bitcast_fusion
  798.8 3.5 copy.242
  808.8 3.3 fusion.66
  812.2 3.5 fusion.29
  822.5 12.9 scatter_custom_fusion.1
  835.4 2.5 convert_element_type.201
  839.6 2.6 all-to-all-start.2
  842.3 66.7 %reduce-scatter.16.cloned.1.call-done = f32[96,256]{1,0:T(8,128)} async-done(((f32[3072,256]{1,0:T(8,128)}), f32[96,256]{1,0:T(8,128)}) %reduce-scatter.16.cloned.1.call-update) | async-done | bytes 98320 | tf_op jit(solution)/shard_map/reduce_scatter | solution.py:332
  910.9 41.7 %all-reduce.25 = (bf16[1536]{0:T(1024)(128)(2,1)S(1)}, bf16[1536]{0:T(1024)(128)(2,1)S(1)}, bf16[1536]{0:T(1024)(128)(2,1)S(1)}, bf16[1536]{0:T(1024)(128)(2,1)S...) all-reduce(f32[1536]{0:T(1024)S(1)} %reshape.371, ...), channel_id=3, replica_groups=mesh['dp'=8,'fsdp'=4] {'dp','fsdp'}, use_global_device_ids=true, to_apply=%region_42.43.clone | all-reduce | flops 26112 | bytes 156672
  955.2 39.7 %all-reduce.26 = (bf16[1536]{0:T(1024)(128)(2,1)S(1)}, bf16[1536]{0:T(1024)(128)(2,1)S(1)}, bf16[1536]{0:T(1024)(128)(2,1)S(1)}, bf16[1536]{0:T(1024)(128)(2,1)S...) all-reduce(bf16[1536]{0:T(1024)(128)(2,1)S(1)} %dynamic-update-slic, ...), channel_id=1, replica_groups=mesh['dp'=8,'fsdp'=4] {'dp','fsdp'}, use_global_device_ids=true, to_apply=%add.8 | all-reduce | flops 9728 | bytes 38912
  999.6 66.4 %all_gather.134 = bf16[256,64]{1,0:T(8,128)(2,1)S(1)} all-gather(bf16[8,64]{1,0:T(8,128)(2,1)S(1)} %copy.255), channel_id=1, replica_groups=mesh['dp'=8,'fsdp'=4] {'dp','fsdp'}, dimensions={0}, use_global_device_ids=true | all-gather | bytes 33792 | tf_op jit(solution)/shard_map/all_gather | solution.py:415
  1067.6 63.5 %all-gather.5 = bf16[32,16,4]{1,2,0:T(4,128)(2,1)S(1)} all-gather(bf16[1,16,4]{1,2,0:T(4,128)(2,1)S(1)} %bitcast.366), channel_id=1, replica_groups=mesh['dp'=8,'fsdp'=4] {'dp','fsdp'}, dimensions={0}, use_global_device_ids=true | all-gather | bytes 4224 | tf_op jit(solution)/shard_map/all_gather | solution.py:406
  1131.9 44.3 %reduce-scatter.28.cloned.1.call-done = f32[16,6]{1,0:T(8,128)} async-done(((f32[512,6]{1,0:T(8,128)}), f32[16,6]{1,0:T(8,128)}) %reduce-scatter.28.cloned.1.call-update) | async-done | bytes 400
  1177.0 64.1 %all-gather.4 = bf16[32,16,6]{1,2,0:T(8,128)(2,1)S(1)} all-gather(bf16[1,16,6]{1,2,0:T(8,128)(2,1)S(1)} %bitcast.365), channel_id=1, replica_groups=mesh['dp'=8,'fsdp'=4] {'dp','fsdp'}, dimensions={0}, use_global_device_ids=true | all-gather | bytes 6336 | tf_op jit(solution)/shard_map/all_gather | solution.py:388
  1242.0 66.5 %reduce-scatter.26.cloned.1.call-done = f32[32,4]{1,0:T(8,128)} async-done(((f32[1024,4]{1,0:T(8,128)}), f32[32,4]{1,0:T(8,128)}) %reduce-scatter.26.cloned.1.call-update) | async-done | bytes 528
  1309.3 63.9 %all-gather.3 = bf16[32,32,4]{1,2,0:T(4,128)(2,1)S(1)} all-gather(bf16[1,32,4]{1,2,0:T(4,128)(2,1)S(1)} %bitcast.367), channel_id=1, replica_groups=mesh['dp'=8,'fsdp'=4] {'dp','fsdp'}, dimensions={0}, use_global_device_ids=true | all-gather | bytes 8448 | tf_op jit(solution)/shard_map/all_gather | solution.py:385
  1373.9 67.4 %reduce-scatter.24.cloned.1.call-done = f32[16,128]{1,0:T(8,128)} async-done(((f32[512,128]{1,0:T(8,128)}), f32[16,128]{1,0:T(8,128)}) %reduce-scatter.24.cloned.1.call-update) | async-done | bytes 8208 | tf_op jit(solution)/shard_map/reduce_scatter | solution.py:345
  1442.0 64.9 %all_gather.132 = bf16[512,128]{1,0:T(8,128)(2,1)S(1)} all-gather(bf16[16,128]{1,0:T(8,128)(2,1)S(1)} %convert_element_type.233), channel_id=1, replica_groups=mesh['dp'=8,'fsdp'=4] {'dp','fsdp'}, dimensions={0}, use_global_device_ids=true | all-gather | bytes 135168 | tf_op jit(solution)/shard_map/all_gather | solution.py:409
  1510.0 46.7 %scatter_custom_fusion.2 = f32[4096,64]{1,0:T(8,128)S(1)} fusion(s32[8192]{0:T(1024)} %bitcast.358, f32[8192,64]{1,0:T(8,128)} %bitcast.331, f32[]{:T(128)} %constant.71.clone.1), kind=kCustom, calls=%fused_computation.93 | custom fusion | flops 524288 | bytes 1049088 | tf_op jit(solution)/shard_map/scatter-add | solution.py:329
  1559.1 79.1 %all_gather.128 = bf16[1536,256]{1,0:T(8,128)(2,1)S(1)} all-gather(bf16[48,256]{1,0:T(8,128)(2,1)S(1)} %convert_element_type.224), channel_id=1, replica_groups=mesh['dp'=8,'fsdp'=4] {'dp','fsdp'}, dimensions={0}, use_global_device_ids=true | all-gather | bytes 811008 | tf_op jit(solution)/shard_map/all_gather | solution.py:397
  1639.5 2.7 reduce-scatter.20.cloned.1.call-done
  1642.9 72.1 %all_gather.126 = bf16[1536,256]{1,0:T(8,128)(2,1)S(1)} all-gather(bf16[48,256]{1,0:T(8,128)(2,1)S(1)} %convert_element_type.219), channel_id=1, replica_groups=mesh['dp'=8,'fsdp'=4] {'dp','fsdp'}, dimensions={0}, use_global_device_ids=true | all-gather | bytes 811008 | tf_op jit(solution)/shard_map/all_gather | solution.py:391
  1716.3 28.1 %reduce-scatter.18.cloned.1.call-done = f32[48,256]{1,0:T(8,128)} async-done(((f32[1536,256]{1,0:T(8,128)}), f32[48,256]{1,0:T(8,128)}) %reduce-scatter.18.cloned.1.call-update) | async-done | bytes 49168 | tf_op jit(solution)/shard_map/reduce_scatter | solution.py:334
  1745.2 73.9 %all_gather.121 = bf16[1536,256]{1,0:T(8,128)(2,1)S(1)} all-gather(bf16[48,256]{1,0:T(8,128)(2,1)S(1)} %convert_element_type.208), channel_id=1, replica_groups=mesh['dp'=8,'fsdp'=4] {'dp','fsdp'}, dimensions={0}, use_global_device_ids=true | all-gather | bytes 811008 | tf_op jit(solution)/shard_map/all_gather | solution.py:376
  1820.3 3.3 convert_element_type.204
  (505 shorter events, 113.5 us)
Async XLA Ops:
  7.2 38.5 %copy-start.117 = (bf16[8]{0:T(256)(128)(2,1)S(1)}, bf16[8]{0:T(256)(128)(2,1)}, u32[]{:S(2)}) copy-start(bf16[8]{0:T(256)(128)(2,1)} %param.40) | copy-start | bytes 52
  7.2 38.8 %copy-start.118 = (bf16[8]{0:T(256)(128)(2,1)S(1)}, bf16[8]{0:T(256)(128)(2,1)}, u32[]{:S(2)}) copy-start(bf16[8]{0:T(256)(128)(2,1)} %param.38) | copy-start | bytes 52
  7.2 39.0 %copy-start.119 = (bf16[48]{0:T(256)(128)(2,1)S(1)}, bf16[48]{0:T(256)(128)(2,1)}, u32[]{:S(2)}) copy-start(bf16[48]{0:T(256)(128)(2,1)} %param.34) | copy-start | bytes 292
  7.2 39.3 %copy-start.120 = (bf16[48]{0:T(256)(128)(2,1)S(1)}, bf16[48]{0:T(256)(128)(2,1)}, u32[]{:S(2)}) copy-start(bf16[48]{0:T(256)(128)(2,1)} %param.32) | copy-start | bytes 292
  7.2 39.5 %copy-start.121 = (bf16[48]{0:T(256)(128)(2,1)S(1)}, bf16[48]{0:T(256)(128)(2,1)}, u32[]{:S(2)}) copy-start(bf16[48]{0:T(256)(128)(2,1)} %param.27) | copy-start | bytes 292
  7.2 39.7 %copy-start.122 = (bf16[48]{0:T(256)(128)(2,1)S(1)}, bf16[48]{0:T(256)(128)(2,1)}, u32[]{:S(2)}) copy-start(bf16[48]{0:T(256)(128)(2,1)} %param.25) | copy-start | bytes 292
  7.3 40.0 %copy-start.123 = (bf16[48]{0:T(256)(128)(2,1)S(1)}, bf16[48]{0:T(256)(128)(2,1)}, u32[]{:S(2)}) copy-start(bf16[48]{0:T(256)(128)(2,1)} %param.28) | copy-start | bytes 292
  7.3 40.2 %copy-start.124 = (bf16[48]{0:T(256)(128)(2,1)S(1)}, bf16[48]{0:T(256)(128)(2,1)}, u32[]{:S(2)}) copy-start(bf16[48]{0:T(256)(128)(2,1)} %param.35) | copy-start | bytes 292
  7.3 710.9 %all-gather.9.cloned.1.call-start = ((), (), s32[]{:S(2)}) async-start(), calls=%async_computation.11 | async-start | bytes 1622016 | tf_op jit(solution)/shard_map/all_gather | solution.py:146
  8.7 82.5 %copy-start.110 = (bf16[32,4]{0,1:T(4,128)(2,1)S(1)}, bf16[32,4]{0,1:T(4,128)(2,1)}, u32[]{:S(2)}) copy-start(bf16[32,4]{0,1:T(4,128)(2,1)} %param.29) | copy-start | bytes 772
  9.6 148.0 %copy-start.111 = (bf16[16,4]{0,1:T(4,128)(2,1)S(1)}, bf16[16,4]{0,1:T(4,128)(2,1)}, u32[]{:S(2)}) copy-start(bf16[16,4]{0,1:T(4,128)(2,1)} %param.36) | copy-start | bytes 388
  9.8 212.7 %copy-start.107 = (bf16[16,6]{0,1:T(8,128)(2,1)S(1)}, bf16[16,6]{0,1:T(8,128)(2,1)}, u32[]{:S(2)}) copy-start(bf16[16,6]{0,1:T(8,128)(2,1)} %param.30) | copy-start | bytes 580
  9.9 278.7 %copy-start.108 = (bf16[8,64]{1,0:T(8,128)(2,1)S(1)}, bf16[8,64]{1,0:T(8,128)(2,1)}, u32[]{:S(2)}) copy-start(bf16[8,64]{1,0:T(8,128)(2,1)} %param.39) | copy-start | bytes 3076
  10.1 347.2 %copy-start.28 = (bf16[4096,64]{0,1:T(8,128)(2,1)S(1)}, bf16[4096,64]{0,1:T(8,128)(2,1)}, u32[]{:S(2)}) copy-start(bf16[4096,64]{0,1:T(8,128)(2,1)} %param.23) | copy-start | bytes 1572868
  11.3 347.1 %copy-start.106 = (bf16[16,128]{1,0:T(8,128)(2,1)S(1)}, bf16[16,128]{1,0:T(8,128)(2,1)}, u32[]{:S(2)}) copy-start(bf16[16,128]{1,0:T(8,128)(2,1)} %param.37) | copy-start | bytes 12292
  22.1 431.2 %copy-start.73 = (s32[4096,1]{0,1:T(1,128)}, s32[4096,1]{0,1:T(1,128)S(1)}, u32[]{:S(2)}) copy-start(s32[4096,1]{0,1:T(1,128)S(1)} %compare_select_fusion.1) | copy-start | bytes 49156
  38.2 385.7 %all-to-all-start = ((s32[32,1,256]{2,1,0:T(1,128)}), s32[32,1,256]{2,1,0:T(1,128)S(1)}, u32[]{:S(2)}, u32[]{:S(2)}) async-start(s32[32,1,256]{2,1,0:T(1,128)} %bitcast.4), calls=%async_computation | async-start | bytes 65536 | tf_op jit(solution)/shard_map/all_to_all | solution.py:137
  89.4 634.1 %copy-start.43 = (f32[3,2,256]{2,1,0:T(2,128)}, f32[3,2,256]{2,1,0:T(2,128)S(1)}, u32[]{:S(2)}) copy-start(f32[3,2,256]{2,1,0:T(2,128)S(1)} %reshape.385) | copy-start | bytes 18436
  90.6 627.6 %copy-start.103 = (f32[3,2,256]{2,1,0:T(2,128)}, f32[3,2,256]{2,1,0:T(2,128)S(1)}, u32[]{:S(2)}) copy-start(f32[3,2,256]{2,1,0:T(2,128)S(1)} %reshape.384) | copy-start | bytes 18436
  157.5 559.5 %copy-start.83 = (bf16[512,4]{0,1:T(4,128)(2,1)}, bf16[512,4]{0,1:T(4,128)(2,1)S(1)}, u32[]{:S(2)}) copy-start(bf16[512,4]{0,1:T(4,128)(2,1)S(1)} %reshape.484) | copy-start | bytes 12292
  157.6 559.7 %copy-start.85 = (bf16[512,4]{0,1:T(4,128)(2,1)}, bf16[512,4]{0,1:T(4,128)(2,1)S(1)}, u32[]{:S(2)}) copy-start(bf16[512,4]{0,1:T(4,128)(2,1)S(1)} %reshape.482) | copy-start | bytes 12292
  288.6 427.5 %copy-start.65 = (bf16[512,6]{0,1:T(8,128)(2,1)}, bf16[512,6]{0,1:T(8,128)(2,1)S(1)}, u32[]{:S(2)}) copy-start(bf16[512,6]{0,1:T(8,128)(2,1)S(1)} %reshape.472) | copy-start | bytes 18436
  423.9 24.1 %copy-start.60 = (s32[8192,1]{0,1:T(1,128)}, s32[8192,1]{0,1:T(1,128)S(1)}, u32[]{:S(2)}) copy-start(s32[8192,1]{0,1:T(1,128)S(1)} %compare_select_fusion) | copy-start | bytes 98308
  448.9 99.8 %copy-start.94 = (bf16[48,256]{1,0:T(8,128)(2,1)S(1)}, bf16[48,256]{1,0:T(8,128)(2,1)}, u32[]{:S(2)}) copy-start(bf16[48,256]{1,0:T(8,128)(2,1)} %param.31) | copy-start | bytes 73732
  448.9 175.5 %copy-start.95 = (bf16[48,256]{1,0:T(8,128)(2,1)S(1)}, bf16[48,256]{1,0:T(8,128)(2,1)}, u32[]{:S(2)}) copy-start(bf16[48,256]{1,0:T(8,128)(2,1)} %param.33) | copy-start | bytes 73732
  450.0 251.2 %all-to-all-start.1 = ((bf16[32,256,64]{1,2,0:T(8,128)(2,1)}), bf16[32,256,64]{1,2,0:T(8,128)(2,1)S(1)}, u32[]{:S(2)}, u32[]{:S(2)}) async-start(bf16[32,256,64]{1,2,0:T(8,128)(2,1)} %broadcast_select_fusion), calls=%async_computation.1 | async-start | bytes 2097152 | tf_op jit(solution)/shard_map/all_to_all | solution.py:141
  452.7 456.3 %reduce-scatter.16.cloned.1.call-start = ((), (), s32[]{:S(2)}) async-start(), calls=%async_computation.12 | async-start | bytes 3244032 | tf_op jit(solution)/shard_map/reduce_scatter | solution.py:332
  738.9 8.2 copy-start.72
  802.4 264.3 %reduce-scatter.30.cloned.1.call-start = ((), (), s32[]{:S(2)}) async-start(), calls=%async_computation.20 | async-start | bytes 270336
  805.9 370.3 %reduce-scatter.28.cloned.1.call-start = ((), (), s32[]{:S(2)}) async-start(), calls=%async_computation.19 | async-start | bytes 270336
  806.4 502.0 %reduce-scatter.26.cloned.1.call-start = ((), (), s32[]{:S(2)}) async-start(), calls=%async_computation.18 | async-start | bytes 540672
  807.6 633.7 %reduce-scatter.24.cloned.1.call-start = ((), (), s32[]{:S(2)}) async-start(), calls=%async_computation.17 | async-start | bytes 270336 | tf_op jit(solution)/shard_map/reduce_scatter | solution.py:345
  808.8 749.5 %reduce-scatter.22.cloned.1.call-start = ((), (), s32[]{:S(2)}) async-start(), calls=%async_computation.16 | async-start | bytes 1622016 | tf_op jit(solution)/shard_map/reduce_scatter | solution.py:341
  812.1 830.0 %reduce-scatter.20.cloned.1.call-start = ((), (), s32[]{:S(2)}) async-start(), calls=%async_computation.15 | async-start | bytes 1622016 | tf_op jit(solution)/shard_map/reduce_scatter | solution.py:339
  815.7 928.7 %reduce-scatter.18.cloned.1.call-start = ((), (), s32[]{:S(2)}) async-start(), calls=%async_computation.14 | async-start | bytes 1622016 | tf_op jit(solution)/shard_map/reduce_scatter | solution.py:334
  822.0 13.3 copy-start.19
  837.8 72.6 %copy-start.38 = (bf16[2,512,128]{2,1,0:T(8,128)(2,1)S(1)}, bf16[2,512,128]{2,1,0:T(8,128)(2,1)}, u32[]{:S(2)}) copy-start(bf16[2,512,128]{2,1,0:T(8,128)(2,1)} %copy-done.37) | copy-start | bytes 786436
  837.8 72.6 %copy-start.59 = (bf16[2,64,512]{2,1,0:T(8,128)(2,1)S(1)}, bf16[2,64,512]{2,1,0:T(8,128)(2,1)}, u32[]{:S(2)}) copy-start(bf16[2,64,512]{2,1,0:T(8,128)(2,1)} %copy-done.58) | copy-start | bytes 393220
  837.9 72.8 %copy-start.112 = (f32[2,64]{1,0:T(2,128)S(1)}, f32[2,64]{1,0:T(2,128)}, u32[]{:S(2)}) copy-start(f32[2,64]{1,0:T(2,128)} %get-tuple-element.142) | copy-start | bytes 1540
  837.9 72.8 %copy-start.113 = (f32[2,64]{1,0:T(2,128)S(1)}, f32[2,64]{1,0:T(2,128)}, u32[]{:S(2)}) copy-start(f32[2,64]{1,0:T(2,128)} %get-tuple-element.172) | copy-start | bytes 1540
  837.9 72.9 %copy-start.89 = (f32[3,2,256]{2,1,0:T(2,128)S(1)}, f32[3,2,256]{2,1,0:T(2,128)}, u32[]{:S(2)}) copy-start(f32[3,2,256]{2,1,0:T(2,128)} %get-tuple-element.102) | copy-start | bytes 18436
  837.9 72.9 %copy-start.102 = (f32[3,2,256]{2,1,0:T(2,128)S(1)}, f32[3,2,256]{2,1,0:T(2,128)}, u32[]{:S(2)}) copy-start(f32[3,2,256]{2,1,0:T(2,128)} %get-tuple-element.201) | copy-start | bytes 18436
  837.9 72.9 %copy-start.90 = (f32[3,2,256]{2,1,0:T(2,128)S(1)}, f32[3,2,256]{2,1,0:T(2,128)}, u32[]{:S(2)}) copy-start(f32[3,2,256]{2,1,0:T(2,128)} %get-tuple-element.144) | copy-start | bytes 18436
  837.9 73.0 %copy-start.91 = (f32[3,2,256]{2,1,0:T(2,128)S(1)}, f32[3,2,256]{2,1,0:T(2,128)}, u32[]{:S(2)}) copy-start(f32[3,2,256]{2,1,0:T(2,128)} %get-tuple-element.100) | copy-start | bytes 18436
  837.9 73.0 %copy-start.92 = (f32[3,2,256]{2,1,0:T(2,128)S(1)}, f32[3,2,256]{2,1,0:T(2,128)}, u32[]{:S(2)}) copy-start(f32[3,2,256]{2,1,0:T(2,128)} %get-tuple-element.146) | copy-start | bytes 18436
  837.9 73.0 %copy-start.109 = (f32[2,128]{1,0:T(2,128)S(1)}, f32[2,128]{1,0:T(2,128)}, u32[]{:S(2)}) copy-start(f32[2,128]{1,0:T(2,128)} %get-tuple-element.203) | copy-start | bytes 3076
  839.6 668.0 %all-to-all-start.2 = ((bf16[32,256,64]{1,2,0:T(8,128)(2,1)}), bf16[32,256,64]{1,2,0:T(8,128)(2,1)S(1)}, u32[]{:S(2)}, u32[]{:S(2)}) async-start(bf16[32,256,64]{1,2,0:T(8,128)(2,1)} %copy.237), calls=%async_computation.2 | async-start | bytes 2097152 | tf_op jit(solution)/shard_map/all_to_all | solution.py:323
  842.2 978.1 %all-gather.11.cloned.1.call-start = ((), (), s32[]{:S(2)}) async-start(), calls=%async_computation.13 | async-start | bytes 1622016 | tf_op jit(solution)/shard_map/all_gather | solution.py:370
  (94 other events, 246.1 us)
Sparse Core Ops, SparseCore 0:
  11.0 57.8 all-gather.8
  802.5 106.3 reduce-scatter.15
  911.2 133.0 reduce-scatter.29
  1046.4 129.7 reduce-scatter.27
  1178.3 130.1 reduce-scatter.25
  1310.7 130.5 reduce-scatter.23
  1446.5 93.0 reduce-scatter.21
  1545.5 96.6 reduce-scatter.19
  1648.0 96.3 reduce-scatter.17
  1747.1 54.8 all-gather.10
where the time goes:
time: 1840 us; the launch traced here: 1830 us
  blocking collectives  1250 us (68%)
  waiting for transfers between devices  277 us (15%)
  local copies, waits for them, and re-layouts  131 us (7%)
  other arithmetic  107 us (6%)
  matrix products  39 us (2%)
    unnamed x3, blocking collectives  122 us
    unnamed x13, waiting for transfers between devices  112 us
    all_gather x1, blocking collectives, on_device(): lax.all_gather(reduceone, ('dp', 'fsdp'), axis=0, tiled=True)  94.8 us
    all_gather x1, blocking collectives, on_device(): lax.all_gather(b_shrink.astype(jnp.bfloat16), ('dp', 'fsdp'), axis=0, til...  79.1 us
    all_gather x1, blocking collectives, on_device(): lax.all_gather(reducetwo, ('dp', 'fsdp'), axis=0, tiled=True)  76.8 us
    all_gather x1, blocking collectives, on_device(): lax.all_gather(expandtwo, ('dp', 'fsdp'), axis=0, tiled=True)  75.8 us
    all_gather x1, blocking collectives, on_device(): lax.all_gather(a_shrink.astype(jnp.bfloat16), ('dp', 'fsdp'), axis=0, til...  73.9 us
    all_gather x1, blocking collectives, on_device(): lax.all_gather(b_expand.astype(jnp.bfloat16), ('dp', 'fsdp'), axis=0, til...  72.1 us
  transfers between devices with their start and end apart: 13, of which 6 were waited for; matrix products, arithmetic and copies ran while one was open for 10% of the time, Pallas kernels for 0%

commit v1 on v0

--- a/solution.py
+++ b/solution.py
@@ -93,6 +93,33 @@
     prob_grad = jnp.sum(pieces * upstream[None], axis=-1)
     score_grad = task_probs * (prob_grad - jnp.sum(task_probs * prob_grad, axis=0, keepdims=True))
     return (piece_grad, score_grad.astype(jnp.bfloat16))
+
+
+def pack_rows(parts, row_tile):
+    width = 256
+    wide = [part for part in parts if part.ndim == 2 and part.shape[1] == width]
+    thin = [part.reshape(-1) for part in parts if part.ndim != 2 or part.shape[1] != width]
+    rest = jnp.concatenate(thin)
+    rest = jnp.pad(rest, (0, -rest.size % (row_tile * width))).reshape(-1, width)
+    return jnp.concatenate(wide + [rest], axis=0)
+
+
+def unpack_rows(whole, parts):
+    devices, rows, width = whole.shape
+    wide_rows = sum(part.shape[0] for part in parts if part.ndim == 2 and part.shape[1] == width)
+    rest = whole[:, wide_rows:].reshape(devices, -1)
+    out = []
+    row = 0
+    place = 0
+    for part in parts:
+        if part.ndim == 2 and part.shape[1] == width:
+            piece = whole[:, row : row + part.shape[0]]
+            row += part.shape[0]
+        else:
+            piece = rest[:, place : place + part.size]
+            place += part.size
+        out.append(piece.reshape((devices * part.shape[0],) + part.shape[1:]))
+    return out
 
 
 def on_device(
@@ -142,37 +169,70 @@
     features = jnp.take(returned.reshape(-1, emb_width), position, axis=0).reshape(
         events, fields * emb_width
     )
-    one_expand, one_inbias, one_shrink, one_outbias, one_gain, one_taskgate, one_sharegate = (
-        lax.all_gather(expandone, ("dp", "fsdp"), axis=0, tiled=True),
-        lax.all_gather(expbiasone, ("dp", "fsdp"), axis=0, tiled=True),
-        lax.all_gather(reduceone, ("dp", "fsdp"), axis=0, tiled=True),
-        lax.all_gather(redbiasone, ("dp", "fsdp"), axis=0, tiled=True),
-        lax.all_gather(normgainone, ("dp", "fsdp"), axis=0, tiled=True),
-        lax.all_gather(taskgateone, ("dp", "fsdp"), axis=0, tiled=True),
-        lax.all_gather(sharegateone, ("dp", "fsdp"), axis=0, tiled=True),
-    )
+    packed = pack_rows(
+        (
+            expandone,
+            reduceone,
+            expandtwo,
+            reducetwo,
+            expbiasone,
+            redbiasone,
+            normgainone,
+            expbiastwo,
+            redbiastwo,
+            normgaintwo,
+            taskgateone,
+            sharegateone,
+            taskgatetwo,
+            towerinner,
+            towerbias,
+            towermiddle,
+            towertail,
+        ),
+        16,
+    )
+    whole = lax.all_gather(packed, "fsdp", axis=0, tiled=False)
+    whole = lax.all_gather(whole, "dp", axis=0, tiled=False)
+    whole = whole.reshape((devices,) + packed.shape)
     (
+        one_expand,
+        one_shrink,
         two_expand,
+        two_shrink,
+        one_inbias,
+        one_outbias,
+        one_gain,
         two_inbias,
-        two_shrink,
         two_outbias,
         two_gain,
+        one_taskgate,
+        one_sharegate,
         two_taskgate,
         inner_full,
         tbias_full,
         middle_full,
         tail_full,
-    ) = (
-        lax.all_gather(expandtwo, ("dp", "fsdp"), axis=0, tiled=True),
-        lax.all_gather(expbiastwo, ("dp", "fsdp"), axis=0, tiled=True),
-        lax.all_gather(reducetwo, ("dp", "fsdp"), axis=0, tiled=True),
-        lax.all_gather(redbiastwo, ("dp", "fsdp"), axis=0, tiled=True),
-        lax.all_gather(normgaintwo, ("dp", "fsdp"), axis=0, tiled=True),
-        lax.all_gather(taskgatetwo, ("dp", "fsdp"), axis=0, tiled=True),
-        lax.all_gather(towerinner, ("dp", "fsdp"), axis=0, tiled=True),
-        lax.all_gather(towerbias, ("dp", "fsdp"), axis=0, tiled=True),
-        lax.all_gather(towermiddle, ("dp", "fsdp"), axis=0, tiled=True),
-        lax.all_gather(towertail, ("dp", "fsdp"), axis=0, tiled=True),
+    ) = unpack_rows(
+        whole,
+        (
+            expandone,
+            reduceone,
+            expandtwo,
+            reducetwo,
+            expbiasone,
+            redbiasone,
+            normgainone,
+            expbiastwo,
+            redbiastwo,
+            normgaintwo,
+            taskgateone,
+            sharegateone,
+            taskgatetwo,
+            towerinner,
+            towerbias,
+            towermiddle,
+            towertail,
+        ),
     )
     in_width = features.shape[1]
     hidden = one_shrink.shape[1]
@@ -328,121 +388,40 @@
         .at[asked_rows.reshape(-1)]
         .add(incoming.reshape(-1, emb_width))
     )
-    all_part = (
-        lax.psum_scatter(low_expand, ("dp", "fsdp"), scatter_dimension=0, tiled=True),
-        lax.psum_scatter(low_inbias, ("dp", "fsdp"), scatter_dimension=0, tiled=True),
-        lax.psum_scatter(low_shrink, ("dp", "fsdp"), scatter_dimension=0, tiled=True),
-        lax.psum_scatter(low_outbias, ("dp", "fsdp"), scatter_dimension=0, tiled=True),
-        lax.psum_scatter(low_gain, ("dp", "fsdp"), scatter_dimension=0, tiled=True),
-        lax.psum_scatter(low_taskgate, ("dp", "fsdp"), scatter_dimension=0, tiled=True),
-        lax.psum_scatter(low_sharegate, ("dp", "fsdp"), scatter_dimension=0, tiled=True),
-        lax.psum_scatter(up_expand, ("dp", "fsdp"), scatter_dimension=0, tiled=True),
-        lax.psum_scatter(up_inbias, ("dp", "fsdp"), scatter_dimension=0, tiled=True),
-        lax.psum_scatter(up_shrink, ("dp", "fsdp"), scatter_dimension=0, tiled=True),
-        lax.psum_scatter(up_outbias, ("dp", "fsdp"), scatter_dimension=0, tiled=True),
-        lax.psum_scatter(up_gain, ("dp", "fsdp"), scatter_dimension=0, tiled=True),
-        lax.psum_scatter(up_taskgate, ("dp", "fsdp"), scatter_dimension=0, tiled=True),
-        lax.psum_scatter(inner_grad, ("dp", "fsdp"), scatter_dimension=0, tiled=True),
-        lax.psum_scatter(tbias_grad, ("dp", "fsdp"), scatter_dimension=0, tiled=True),
-        lax.psum_scatter(middle_grad, ("dp", "fsdp"), scatter_dimension=0, tiled=True),
-        lax.psum_scatter(tail_grad, ("dp", "fsdp"), scatter_dimension=0, tiled=True),
-    )
-    (
-        a_expand,
-        a_inbias,
-        a_shrink,
-        a_outbias,
-        a_gain,
-        a_taskgate,
-        a_sharegate,
-        b_expand,
-        b_inbias,
-        b_shrink,
-        b_outbias,
-        b_gain,
-        b_taskgate,
-        b_inner,
-        b_tbias,
-        b_middle,
-        b_tail,
-    ) = all_part
-    all_done = (
-        lax.all_gather(a_expand.astype(jnp.bfloat16), ("dp", "fsdp"), axis=0, tiled=True).astype(
-            a_expand.dtype
-        ),
-        lax.all_gather(a_inbias.astype(jnp.bfloat16), ("dp", "fsdp"), axis=0, tiled=True).astype(
-            a_inbias.dtype
-        ),
-        lax.all_gather(a_shrink.astype(jnp.bfloat16), ("dp", "fsdp"), axis=0, tiled=True).astype(
-            a_shrink.dtype
-        ),
-        lax.all_gather(a_outbias.astype(jnp.bfloat16), ("dp", "fsdp"), axis=0, tiled=True).astype(
-            a_outbias.dtype
-        ),
-        lax.all_gather(a_gain.astype(jnp.bfloat16), ("dp", "fsdp"), axis=0, tiled=True).astype(
-            a_gain.dtype
-        ),
-        lax.all_gather(a_taskgate.astype(jnp.bfloat16), ("dp", "fsdp"), axis=0, tiled=True).astype(
-            a_taskgate.dtype
-        ),
-        lax.all_gather(a_sharegate.astype(jnp.bfloat16), ("dp", "fsdp"), axis=0, tiled=True).astype(
-            a_sharegate.dtype
-        ),
-        lax.all_gather(b_expand.astype(jnp.bfloat16), ("dp", "fsdp"), axis=0, tiled=True).astype(
-            b_expand.dtype
-        ),
-        lax.all_gather(b_inbias.astype(jnp.bfloat16), ("dp", "fsdp"), axis=0, tiled=True).astype(
-            b_inbias.dtype
-        ),
-        lax.all_gather(b_shrink.astype(jnp.bfloat16), ("dp", "fsdp"), axis=0, tiled=True).astype(
-            b_shrink.dtype
-        ),
-        lax.all_gather(b_outbias.astype(jnp.bfloat16), ("dp", "fsdp"), axis=0, tiled=True).astype(
-            b_outbias.dtype
-        ),
-        lax.all_gather(b_gain.astype(jnp.bfloat16), ("dp", "fsdp"), axis=0, tiled=True).astype(
-            b_gain.dtype
-        ),
-        lax.all_gather(b_taskgate.astype(jnp.bfloat16), ("dp", "fsdp"), axis=0, tiled=True).astype(
-            b_taskgate.dtype
-        ),
-        lax.all_gather(b_inner.astype(jnp.bfloat16), ("dp", "fsdp"), axis=0, tiled=True).astype(
-            b_inner.dtype
-        ),
-        lax.all_gather(b_tbias.astype(jnp.bfloat16), ("dp", "fsdp"), axis=0, tiled=True).astype(
-            b_tbias.dtype
-        ),
-        lax.all_gather(b_middle.astype(jnp.bfloat16), ("dp", "fsdp"), axis=0, tiled=True).astype(
-            b_middle.dtype
-        ),
-        lax.all_gather(b_tail.astype(jnp.bfloat16), ("dp", "fsdp"), axis=0, tiled=True).astype(
-            b_tail.dtype
-        ),
-    )
-    lower_done = all_done[:7]
-    upper_done = all_done[7:]
-    return (
-        logits,
-        x_grad,
-        table_grad,
-        lower_done[0],
-        lower_done[1],
-        lower_done[2],
-        lower_done[3],
-        lower_done[4],
-        lower_done[5],
-        lower_done[6],
-        upper_done[0],
-        upper_done[1],
-        upper_done[2],
-        upper_done[3],
-        upper_done[4],
-        upper_done[5],
-        upper_done[6],
-        upper_done[7],
-        upper_done[8],
-        upper_done[9],
-    )
+    grads = (
+        low_expand,
+        low_inbias,
+        low_shrink,
+        low_outbias,
+        low_gain,
+        low_taskgate,
+        low_sharegate,
+        up_expand,
+        up_inbias,
+        up_shrink,
+        up_outbias,
+        up_gain,
+        up_taskgate,
+        inner_grad,
+        tbias_grad,
+        middle_grad,
+        tail_grad,
+    )
+    sizes = [grad.size for grad in grads]
+    width = one_shrink.shape[1]
+    chunk = 16 * devices * width
+    flat = jnp.concatenate([grad.astype(jnp.bfloat16).reshape(-1) for grad in grads])
+    flat = jnp.pad(flat, (0, -flat.size % chunk)).reshape(-1, width)
+    part = lax.psum_scatter(flat, "dp", scatter_dimension=0, tiled=True)
+    part = lax.psum_scatter(part, "fsdp", scatter_dimension=0, tiled=True)
+    total = lax.all_gather(part, "fsdp", axis=0, tiled=True)
+    total = lax.all_gather(total, "dp", axis=0, tiled=True).reshape(-1)
+    done = []
+    start = 0
+    for grad, size in zip(grads, sizes):
+        done.append(total[start : start + size].reshape(grad.shape).astype(jnp.float32))
+        start += size
+    return (logits, x_grad, table_grad, *done)
 
 
 def solution(mesh):

time: 1840 us -> 591 us (0.32)
  blocking collectives: 1250 us -> 63.8 us
  waiting for transfers between devices: 277 us -> 106 us
  local copies, waits for them, and re-layouts: 131 us -> 229 us
    all_gather x16 -> x2, blocking collectives: 1120 us -> 34.7 us  [the longest x1 18 us: on_device(): whole = lax.all_gather(packed, 'fsdp', axis=0, tiled=False)]
    unnamed x3 -> x0, blocking collectives: 122 us -> none
    unnamed x13 -> x4, waiting for transfers between devices: 112 us -> 0.07 us
    reduce_scatter x5 -> x2, waiting for transfers between devices: 165 us -> 75.2 us  [the longest x1 51.2 us: on_device(): part = lax.psum_scatter(flat, 'dp', scatter_dimension=0, tiled=True)]
    unnamed x310 -> x284, local copies, waits for them, and re-layouts: 21.9 us -> 77.9 us
    all_to_all x0 -> x1, blocking collectives: none -> 29 us  [on_device(): lax.all_to_all(outgoing.astype(jnp.bfloat16), ('dp', 'fsdp'), split_axis=...]
    all_to_all x1, waiting for transfers between devices: 0.01 us -> 23.5 us  [on_device(): lax.all_to_all(found_rows, ('dp', 'fsdp'), split_axis=0, concat_axis=0, t...]
    convert_element_type x5 -> x33, local copies, waits for them, and re-layouts: 2.29 us -> 23.4 us  [the longest x14 14.4 us: on_device(): grad.astype(jnp.bfloat16).reshape(-1)]
  transfers between devices with their start and end apart: 13 -> 6, of which waited for: 6 -> 4; matrix products, arithmetic and copies ran while one was open for 10% -> 26% of each run, Pallas kernels for 0% -> 0%
where the time goes in v1:
time: 591 us; the launch traced here: 581 us
  local copies, waits for them, and re-layouts  229 us (39%)
  other arithmetic  115 us (19%)
  waiting for transfers between devices  106 us (18%)
  blocking collectives  63.8 us (11%)
  matrix products  42.1 us (7%)
  between operations  15.7 us (3%)
  starting transfers between devices  9.8 us (2%)
    unnamed x284, local copies, waits for them, and re-layouts  77.9 us
    scatter-add x1, other arithmetic, on_device(): table_grad = jnp.zeros((embed_table.shape[0], emb_width), jnp.float32).at...  53.9 us
    reduce_scatter x1, waiting for transfers between devices, on_device(): part = lax.psum_scatter(flat, 'dp', scatter_dimension=0, tiled=True)  51.2 us
    all_to_all x1, blocking collectives, on_device(): lax.all_to_all(outgoing.astype(jnp.bfloat16), ('dp', 'fsdp'), split_axis=...  29 us
    gather x2, local copies, waits for them, and re-layouts, on_device(): jnp.take(embed_table, asked_rows.reshape(-1), axis=0)  24.8 us
    reduce_scatter x1, waiting for transfers between devices, on_device(): part = lax.psum_scatter(part, 'fsdp', scatter_dimension=0, tiled=True)  24 us
    all_to_all x1, waiting for transfers between devices, on_device(): lax.all_to_all(found_rows, ('dp', 'fsdp'), split_axis=0, concat_axis=0, t...  23.5 us
    all_gather x1, blocking collectives, on_device(): whole = lax.all_gather(packed, 'fsdp', axis=0, tiled=False)  18 us
  transfers between devices with their start and end apart: 6, of which 4 were waited for; matrix products, arithmetic and copies ran while one was open for 26% of the time, Pallas kernels for 0%

profile of v1, /device:TPU:0, one launch (start us, length us, event | category | flops | bytes accessed | tf_op | source)
XLA Modules:
  0.0 581.3 jit_solution(4896258213192736884)
XLA Ops:
  10.6 6.1 %concatenate.29 = bf16[3152]{0:T(1024)(128)(2,1)S(1)} concatenate(bf16[48]{0:T(256)(128)(2,1)} %param.25, bf16[48]{0:T(256)(128)(2,1)} %param.27, bf16[48]{0:T(256)(128)(2,1)} %param.28, bf16[48]{0:T(256)(128)(2,1)} %param.32, bf16[48]{0:T(256)(128)(2,1)} %param.34, bf16[48]{0:T(256)(128)(2,1)} %param.35, bf16[128]{0:T(256)(128)(2,1)S(1)} %reshape.500, ...), dimensions={0} | concatenate | bytes 12608 | tf_op jit(solution)/shard_map/concatenate | solution.py:102
  19.8 18.0 %all-gather = bf16[1024,256]{1,0:T(8,128)(2,1)} all-gather(bf16[256,256]{1,0:T(8,128)(2,1)S(1)} %constant_dynamic-update-slice_fusion), channel_id=2, replica_groups=mesh['dp'=8,'fsdp'=4] {'fsdp'}, dimensions={0}, use_global_device_ids=true | all-gather | bytes 655360 | tf_op jit(solution)/shard_map/all_gather | solution.py:194
  41.1 9.2 %reduce-window.6 = s32[32,32,128]{2,1,0:T(8,128)S(1)} reduce-window(s32[32,32,128]{2,1,0:T(8,128)S(1)} %fusion.29, s32[]{:T(128)} %constant.70.clone.1), window={size=1x1x128 pad=0_0x0_0x127_0}, to_apply=%region_0.0 | reduce-window | flops 16646144 | bytes 1048580 | tf_op jit(solution)/shard_map/reduce-window
  51.9 16.1 %scatter_custom_fusion = s32[8192]{0:T(1024)} fusion(s32[4096]{0:T(1024)S(1)} %bitcast.309, s32[4096]{0:T(1024)S(1)} %reshape.563, s32[]{:T(128)} %constant.70.clone.1), kind=kCustom, calls=%fused_computation.150 | custom fusion | bytes 32772 | tf_op jit(solution)/shard_map/scatter | solution.py:161
  68.0 6.5 %all-to-all-start = ((s32[32,1,256]{2,1,0:T(1,128)}), s32[32,1,256]{2,1,0:T(1,128)S(1)}, u32[]{:S(2)}, u32[]{:S(2)}) async-start(s32[32,1,256]{2,1,0:T(1,128)} %bitcast.5), calls=%async_computation | async-start | bytes 65536 | tf_op jit(solution)/shard_map/all_to_all | solution.py:164
  75.0 6.8 %all-to-all-done = s32[32,1,256]{2,1,0:T(1,128)S(1)} async-done(((s32[32,1,256]{2,1,0:T(1,128)}), s32[32,1,256]{2,1,0:T(1,128)S(1)}, u32[]{:S(2)}, u32[]{:S(2)}) %all-to-all-start) | async-done | bytes 32800 | tf_op jit(solution)/shard_map/all_to_all | solution.py:164
  82.5 24.0 %gather_fusion = bf16[8192,64]{1,0:T(8,128)(2,1)S(1)} fusion(bf16[4096,64]{1,0:T(8,128)(2,1)S(1)} %copy.233, s32[8192]{0:T(1024)S(1)} %broadcast_clamp_fusion), kind=kCustom, calls=%fused_computation | custom fusion | bytes 2129920 | tf_op jit(solution)/shard_map/jit(_take)/gather | solution.py:165
  108.4 2.6 all-to-all-start.1
  112.6 23.5 %all-to-all-done.1 = bf16[32,256,64]{1,2,0:T(8,128)(2,1)S(1)} async-done(((bf16[32,256,64]{1,2,0:T(8,128)(2,1)}), bf16[32,256,64]{1,2,0:T(8,128)(2,1)S(1)}, u32[]{:S(2)}, u32[]{:S(2)}) %all-to-all-start.1) | async-done | bytes 1048608 | tf_op jit(solution)/shard_map/all_to_all | solution.py:168
  137.2 12.1 %gather_fusion.1 = bf16[4096,64]{1,0:T(8,128)(2,1)S(1)} fusion(bf16[8192,64]{1,0:T(8,128)(2,1)S(1)} %bitcast.258, s32[4096]{0:T(1024)S(1)} %broadcast_clamp_fusion.1), kind=kCustom, calls=%fused_computation.1 | custom fusion | bytes 1064960 | tf_op jit(solution)/shard_map/jit(_take)/gather | solution.py:169
  167.6 3.0 fusion.11
  173.6 3.0 multiply_reduce_fusion.6
  177.4 2.2 slice_bitcast_fusion.7
  188.9 4.2 fusion.3
  209.8 2.0 copy.252
  211.8 2.0 copy.251
  213.9 5.1 multiply_reduce_fusion.13
  227.7 2.8 slice_bitcast_fusion.3
  230.9 2.3 multiply_reduce_fusion
  235.9 4.4 fusion.55
  242.7 2.6 fusion.67
  247.9 2.3 copy.271
  250.3 2.8 copy.316
  253.1 2.8 copy.318
  258.1 2.7 maximum_add_fusion.1
  262.0 2.0 copy.256
  264.1 2.0 copy.258
  266.1 2.1 copy.257
  268.1 2.9 multiply_reduce_fusion.10
  274.1 2.4 multiply_reduce_fusion.1
  279.9 3.6 fusion.56
  290.7 2.2 fusion.18
  293.0 2.1 copy.267
  300.5 13.4 %dynamic-update-slice.2 = bf16[2066944]{0:T(1024)(128)(2,1)} dynamic-update-slice(bf16[2066944]{0:T(1024)(128)(2,1)} %dynamic-update-slice.1, bf16[393216]{0:T(1024)(128)(2,1)} %bitcast.279, s32[]{} %constant.105) | dynamic-update-slice | bytes 1572868
  319.7 13.1 %dynamic-update-slice.7 = bf16[2066944]{0:T(1024)(128)(2,1)} dynamic-update-slice(bf16[2066944]{0:T(1024)(128)(2,1)} %dynamic-update-slice.6, bf16[393216]{0:T(1024)(128)(2,1)S(1)} %bitcast.278, s32[]{} %constant.110) | dynamic-update-slice | bytes 1572868
  343.7 4.4 pad.9
  348.1 7.2 %reshape.519 = bf16[8192,256]{1,0:T(8,128)(2,1)} reshape(bf16[2097152]{0:T(1024)(128)(2,1)} %pad.9) | data formatting | bytes 8388608 | tf_op jit(solution)/shard_map/reshape | solution.py:414
  355.3 51.2 %reduce-scatter.3.cloned.1.call-done = bf16[1024,256]{1,0:T(8,128)(2,1)} async-done(((bf16[8192,256]{1,0:T(8,128)(2,1)}), bf16[1024,256]{1,0:T(8,128)(2,1)}) %reduce-scatter.3.cloned.1.call-update) | async-done | bytes 524304 | tf_op jit(solution)/shard_map/reduce_scatter | solution.py:415
  406.6 24.0 %reduce-scatter.5.cloned.1.call-done = bf16[256,256]{1,0:T(8,128)(2,1)} async-done(((bf16[1024,256]{1,0:T(8,128)(2,1)}), bf16[256,256]{1,0:T(8,128)(2,1)}) %reduce-scatter.5.cloned.1.call-update) | async-done | bytes 131088 | tf_op jit(solution)/shard_map/reduce_scatter | solution.py:416
  430.6 16.8 %all_gather.22 = bf16[1024,256]{1,0:T(8,128)(2,1)} all-gather(bf16[256,256]{1,0:T(8,128)(2,1)} %reduce-scatter.5.cloned.1.call-done), channel_id=1, replica_groups=mesh['dp'=8,'fsdp'=4] {'fsdp'}, dimensions={0}, use_global_device_ids=true | all-gather | bytes 655360 | tf_op jit(solution)/shard_map/all_gather | solution.py:417
  448.2 2.4 convolution_bitcast_fusion
  451.4 13.0 %scatter_custom_fusion.1 = f32[8192,64]{1,0:T(8,128)} fusion(s32[4096]{0:T(1024)} %bitcast.311, f32[4096,64]{1,0:T(8,128)S(1)} %reshape.571, f32[]{:T(128)} %constant.78.clone.1), kind=kCustom, calls=%fused_computation.49 | custom fusion | bytes 2097664 | tf_op jit(solution)/shard_map/scatter | solution.py:380
  464.4 2.4 convert_element_type.365
  467.6 29.0 %all_to_all.19 = bf16[32,256,64]{1,2,0:T(8,128)(2,1)S(1)} all-to-all(bf16[32,256,64]{1,2,0:T(8,128)(2,1)S(1)} %copy.262), channel_id=1, replica_groups=mesh['dp'=8,'fsdp'=4] {'dp','fsdp'}, dimensions={0} | all-to-all | bytes 2097152 | tf_op jit(solution)/shard_map/all_to_all | solution.py:383
  496.7 2.5 copy.305
  499.1 53.9 %scatter_custom_fusion.2 = f32[4096,64]{1,0:T(8,128)S(1)} fusion(s32[8192]{0:T(1024)} %bitcast.307, f32[8192,64]{1,0:T(8,128)} %bitcast.270, f32[]{:T(128)} %constant.78.clone.1), kind=kCustom, calls=%fused_computation.100 | custom fusion | flops 524288 | bytes 1049088 | tf_op jit(solution)/shard_map/scatter-add | solution.py:389
  568.9 3.3 slice_convert_fusion
  572.2 2.3 slice_convert_fusion.1
  (460 shorter events, 138.2 us)
Async XLA Ops:
  7.2 144.6 %all-gather.7.cloned.1.call-start = ((), (), s32[]{:S(2)}) async-start(), calls=%async_computation.8 | async-start | bytes 4718592 | tf_op jit(solution)/shard_map/all_gather | solution.py:195
  37.8 36.7 %copy-start.41 = (bf16[4096,64]{0,1:T(8,128)(2,1)S(1)}, bf16[4096,64]{0,1:T(8,128)(2,1)}, u32[]{:S(2)}) copy-start(bf16[4096,64]{0,1:T(8,128)(2,1)} %param.23) | copy-start | bytes 1572868
  51.9 60.7 %copy-start.86 = (s32[4096,1]{0,1:T(1,128)}, s32[4096,1]{0,1:T(1,128)S(1)}, u32[]{:S(2)}) copy-start(s32[4096,1]{0,1:T(1,128)S(1)} %compare_select_fusion.1) | copy-start | bytes 49156
  68.0 13.8 %all-to-all-start = ((s32[32,1,256]{2,1,0:T(1,128)}), s32[32,1,256]{2,1,0:T(1,128)S(1)}, u32[]{:S(2)}, u32[]{:S(2)}) async-start(s32[32,1,256]{2,1,0:T(1,128)} %bitcast.5), calls=%async_computation | async-start | bytes 65536 | tf_op jit(solution)/shard_map/all_to_all | solution.py:164
  107.3 5.3 copy-start.68
  108.4 27.7 %all-to-all-start.1 = ((bf16[32,256,64]{1,2,0:T(8,128)(2,1)}), bf16[32,256,64]{1,2,0:T(8,128)(2,1)S(1)}, u32[]{:S(2)}, u32[]{:S(2)}) async-start(bf16[32,256,64]{1,2,0:T(8,128)(2,1)} %broadcast_select_fusion), calls=%async_computation.1 | async-start | bytes 2097152 | tf_op jit(solution)/shard_map/all_to_all | solution.py:168
  111.1 295.5 %reduce-scatter.3.cloned.1.call-start = ((), (), s32[]{:S(2)}) async-start(), calls=%async_computation.5 | async-start | bytes 4718592 | tf_op jit(solution)/shard_map/reduce_scatter | solution.py:415
  158.4 14.6 %copy-start.54 = (f32[3,2,256]{2,1,0:T(2,128)}, f32[3,2,256]{2,1,0:T(2,128)S(1)}, u32[]{:S(2)}) copy-start(f32[3,2,256]{2,1,0:T(2,128)S(1)} %reshape.521) | copy-start | bytes 18436
  160.5 10.2 %copy-start.109 = (f32[3,2,256]{2,1,0:T(2,128)}, f32[3,2,256]{2,1,0:T(2,128)S(1)}, u32[]{:S(2)}) copy-start(f32[3,2,256]{2,1,0:T(2,128)S(1)} %reshape.520) | copy-start | bytes 18436
  161.0 9.7 %copy-start.35 = (bf16[512,4]{1,0:T(8,128)(2,1)}, bf16[512,4]{1,0:T(8,128)(2,1)S(1)}, u32[]{:S(2)}) copy-start(bf16[512,4]{1,0:T(8,128)(2,1)S(1)} %squeeze.49) | copy-start | bytes 12292
  161.3 9.4 %copy-start.37 = (bf16[512,4]{1,0:T(8,128)(2,1)}, bf16[512,4]{1,0:T(8,128)(2,1)S(1)}, u32[]{:S(2)}) copy-start(bf16[512,4]{1,0:T(8,128)(2,1)S(1)} %squeeze.45) | copy-start | bytes 12292
  164.3 6.4 %copy-start.92 = (f32[512]{0:T(512)}, f32[512]{0:T(512)S(1)}, u32[]{:S(2)}) copy-start(f32[512]{0:T(512)S(1)} %get-tuple-element.174) | copy-start | bytes 6148
  164.3 6.3 %copy-start.98 = (f32[512]{0:T(512)}, f32[512]{0:T(512)S(1)}, u32[]{:S(2)}) copy-start(f32[512]{0:T(512)S(1)} %fusion.35) | copy-start | bytes 6148
  188.3 8.3 %copy-start.85 = (f32[4,512]{1,0:T(4,128)}, f32[4,512]{1,0:T(4,128)S(1)}, u32[]{:S(2)}) copy-start(f32[4,512]{1,0:T(4,128)S(1)} %fusion.42) | copy-start | bytes 24580
  213.9 6.0 %copy-start.40 = (bf16[256,4]{1,0:T(8,128)(2,1)S(1)}, bf16[256,4]{1,0:T(8,128)(2,1)}, u32[]{:S(2)}) copy-start(bf16[256,4]{1,0:T(8,128)(2,1)} %squeeze.44) | copy-start | bytes 6148
  213.9 7.1 %copy-start.50 = (f32[4,512]{1,0:T(4,128)S(1)}, f32[4,512]{1,0:T(4,128)}, u32[]{:S(2)}) copy-start(f32[4,512]{1,0:T(4,128)} %copy-done.49) | copy-start | bytes 24580
  213.9 7.1 %copy-start.81 = (f32[512]{0:T(512)S(1)}, f32[512]{0:T(512)}, u32[]{:S(2)}) copy-start(f32[512]{0:T(512)} %copy-done.80) | copy-start | bytes 6148
  213.9 7.0 %copy-start.91 = (f32[512]{0:T(512)S(1)}, f32[512]{0:T(512)}, u32[]{:S(2)}) copy-start(f32[512]{0:T(512)} %copy-done.90) | copy-start | bytes 6148
  213.9 7.1 %copy-start.30 = (bf16[512,256]{1,0:T(8,128)(2,1)S(1)}, bf16[512,256]{1,0:T(8,128)(2,1)}, u32[]{:S(2)}) copy-start(bf16[512,256]{1,0:T(8,128)(2,1)} %copy.242) | copy-start | bytes 786436
  213.9 7.8 %copy-start.39 = (bf16[256,4]{1,0:T(8,128)(2,1)S(1)}, bf16[256,4]{1,0:T(8,128)(2,1)}, u32[]{:S(2)}) copy-start(bf16[256,4]{1,0:T(8,128)(2,1)} %squeeze.54) | copy-start | bytes 6148
  213.9 8.9 %copy-start.115 = (bf16[2,64]{1,0:T(2,128)(2,1)S(1)}, bf16[2,64]{1,0:T(2,128)(2,1)}, u32[]{:S(2)}) copy-start(bf16[2,64]{1,0:T(2,128)(2,1)} %get-tuple-element.117) | copy-start | bytes 772
  213.9 8.9 %copy-start.120 = (bf16[2,64]{1,0:T(2,128)(2,1)S(1)}, bf16[2,64]{1,0:T(2,128)(2,1)}, u32[]{:S(2)}) copy-start(bf16[2,64]{1,0:T(2,128)(2,1)} %get-tuple-element.115) | copy-start | bytes 772
  247.9 8.0 %copy-start.114 = (bf16[3,2,256]{2,1,0:T(2,128)(2,1)S(1)}, bf16[3,2,256]{2,1,0:T(2,128)(2,1)}, u32[]{:S(2)}) copy-start(bf16[3,2,256]{2,1,0:T(2,128)(2,1)} %get-tuple-element.197) | copy-start | bytes 9220
  247.9 8.6 %copy-start.106 = (bf16[3,2,256]{2,1,0:T(2,128)(2,1)S(1)}, bf16[3,2,256]{2,1,0:T(2,128)(2,1)}, u32[]{:S(2)}) copy-start(bf16[3,2,256]{2,1,0:T(2,128)(2,1)} %get-tuple-element.119) | copy-start | bytes 9220
  247.9 9.2 %copy-start.107 = (bf16[256,4]{0,1:T(4,128)(2,1)S(1)}, bf16[256,4]{0,1:T(4,128)(2,1)}, u32[]{:S(2)}) copy-start(bf16[256,4]{0,1:T(4,128)(2,1)} %convolution_convert_fusion.10) | copy-start | bytes 6148
  247.9 9.2 %copy-start.108 = (bf16[256,4]{0,1:T(4,128)(2,1)S(1)}, bf16[256,4]{0,1:T(4,128)(2,1)}, u32[]{:S(2)}) copy-start(bf16[256,4]{0,1:T(4,128)(2,1)} %convolution_convert_fusion.9) | copy-start | bytes 6148
  247.9 10.2 %copy-start.117 = (f32[3]{0:T(128)S(1)}, f32[3]{0:T(128)}, u32[]{:S(2)}) copy-start(f32[3]{0:T(128)} %pad.21.clone) | copy-start | bytes 40
  260.8 7.3 %copy-start.59 = (f32[4,512]{1,0:T(4,128)S(1)}, f32[4,512]{1,0:T(4,128)}, u32[]{:S(2)}) copy-start(f32[4,512]{1,0:T(4,128)} %copy-done.58) | copy-start | bytes 24580
  260.8 7.3 %copy-start.61 = (f32[4,512]{1,0:T(4,128)S(1)}, f32[4,512]{1,0:T(4,128)}, u32[]{:S(2)}) copy-start(f32[4,512]{1,0:T(4,128)} %copy-done.60) | copy-start | bytes 24580
  277.2 6.3 %copy-start.94 = (bf16[4,512]{1,0:T(4,128)(2,1)}, bf16[4,512]{1,0:T(4,128)(2,1)S(1)}, u32[]{:S(2)}) copy-start(bf16[4,512]{1,0:T(4,128)(2,1)S(1)} %multiply_convert_fusion.5) | copy-start | bytes 12292
  296.7 23.0 %copy-start.29 = (bf16[192,2,8,128]{3,1,2,0:T(2,128)(2,1)S(1)}, bf16[192,2,8,128]{3,1,2,0:T(2,128)(2,1)}, u32[]{:S(2)}) copy-start(bf16[192,2,8,128]{3,1,2,0:T(2,128)(2,1)} %copy.316) | copy-start | bytes 2359300
  297.7 35.1 %copy-start.104 = (bf16[1536]{0:T(1024)(128)(2,1)S(1)}, bf16[1536]{0:T(1024)(128)(2,1)}, u32[]{:S(2)}) copy-start(bf16[1536]{0:T(1024)(128)(2,1)} %convert_element_type.381) | copy-start | bytes 9220
  297.7 36.6 %copy-start.28 = (bf16[192,2,8,128]{3,1,2,0:T(2,128)(2,1)S(1)}, bf16[192,2,8,128]{3,1,2,0:T(2,128)(2,1)}, u32[]{:S(2)}) copy-start(bf16[192,2,8,128]{3,1,2,0:T(2,128)(2,1)} %copy.318) | copy-start | bytes 2359300
  299.0 36.3 %copy-start.103 = (bf16[1536]{0:T(1024)(128)(2,1)S(1)}, bf16[1536]{0:T(1024)(128)(2,1)}, u32[]{:S(2)}) copy-start(bf16[1536]{0:T(1024)(128)(2,1)} %convert_element_type.384) | copy-start | bytes 9220
  299.0 37.7 %copy-start.102 = (bf16[1536]{0:T(1024)(128)(2,1)S(1)}, bf16[1536]{0:T(1024)(128)(2,1)}, u32[]{:S(2)}) copy-start(bf16[1536]{0:T(1024)(128)(2,1)} %convert_element_type.386) | copy-start | bytes 9220
  299.0 39.1 %copy-start.105 = (bf16[2048]{0:T(1024)(128)(2,1)S(1)}, bf16[2048]{0:T(1024)(128)(2,1)}, u32[]{:S(2)}) copy-start(bf16[2048]{0:T(1024)(128)(2,1)} %convert_element_type.387) | copy-start | bytes 12292
  299.0 39.7 %copy-start.70 = (bf16[2,256,128]{2,1,0:T(8,128)(2,1)S(1)}, bf16[2,256,128]{2,1,0:T(8,128)(2,1)}, u32[]{:S(2)}) copy-start(bf16[2,256,128]{2,1,0:T(8,128)(2,1)} %convolution_convert_fusion.4) | copy-start | bytes 393220
  299.0 40.4 %copy-start.118 = (bf16[2,128]{1,0:T(2,128)(2,1)S(1)}, bf16[2,128]{1,0:T(2,128)(2,1)}, u32[]{:S(2)}) copy-start(bf16[2,128]{1,0:T(2,128)(2,1)} %get-tuple-element.199) | copy-start | bytes 1540
  299.0 41.8 %copy-start.69 = (bf16[16384]{0:T(1024)(128)(2,1)S(1)}, bf16[16384]{0:T(1024)(128)(2,1)}, u32[]{:S(2)}) copy-start(bf16[16384]{0:T(1024)(128)(2,1)} %convert_element_type.392) | copy-start | bytes 98308
  299.0 43.3 %copy-start.119 = (bf16[256]{0:T(256)(128)(2,1)S(1)}, bf16[256]{0:T(256)(128)(2,1)}, u32[]{:S(2)}) copy-start(bf16[256]{0:T(256)(128)(2,1)} %convert_element_type.394) | copy-start | bytes 1540
  355.2 92.2 %copy-start.38 = (bf16[512,4]{1,0:T(8,128)(2,1)S(1)}, bf16[512,4]{1,0:T(8,128)(2,1)}, u32[]{:S(2)}) copy-start(bf16[512,4]{1,0:T(8,128)(2,1)} %copy-done.37) | copy-start | bytes 12292
  355.2 92.2 %copy-start.97 = (bf16[4,512]{1,0:T(4,128)(2,1)S(1)}, bf16[4,512]{1,0:T(4,128)(2,1)}, u32[]{:S(2)}) copy-start(bf16[4,512]{1,0:T(4,128)(2,1)} %copy-done.96) | copy-start | bytes 12292
  355.2 92.5 %copy-start.36 = (bf16[512,4]{1,0:T(8,128)(2,1)S(1)}, bf16[512,4]{1,0:T(8,128)(2,1)}, u32[]{:S(2)}) copy-start(bf16[512,4]{1,0:T(8,128)(2,1)} %copy-done.35) | copy-start | bytes 12292
  355.2 92.5 %copy-start.95 = (bf16[4,512]{1,0:T(4,128)(2,1)S(1)}, bf16[4,512]{1,0:T(4,128)(2,1)}, u32[]{:S(2)}) copy-start(bf16[4,512]{1,0:T(4,128)(2,1)} %copy-done.94) | copy-start | bytes 12292
  355.3 92.9 %copy-start.34 = (bf16[32,96,256]{2,1,0:T(8,128)(2,1)S(1)}, bf16[32,96,256]{2,1,0:T(8,128)(2,1)}, u32[]{:S(2)}) copy-start(bf16[32,96,256]{2,1,0:T(8,128)(2,1)} %copy-done.33) | copy-start | bytes 4718596
  355.3 75.3 %reduce-scatter.5.cloned.1.call-start = ((), (), s32[]{:S(2)}) async-start(), calls=%async_computation.6 | async-start | bytes 655360 | tf_op jit(solution)/shard_map/reduce_scatter | solution.py:416
  406.6 148.0 %all-gather.5.cloned.1.call-start = ((), (), s32[]{:S(2)}) async-start(), calls=%async_computation.7 | async-start | bytes 4718592 | tf_op jit(solution)/shard_map/all_gather | solution.py:418
  451.0 13.4 %copy-start.21 = (f32[512,512]{1,0:T(8,128)}, f32[512,512]{1,0:T(8,128)S(1)}, u32[]{:S(2)}) copy-start(f32[512,512]{1,0:T(8,128)S(1)} %fusion.19) | copy-start | bytes 3145732
  (82 other events, 214.2 us)
Sparse Core Ops, SparseCore 0:
  37.9 38.5 all-gather.6
  355.4 51.1 reduce-scatter.2
  408.9 21.6 reduce-scatter.4
  447.5 45.3 all-gather.4
